TPU v7x, 32 devices: a whole 2x2x4 slice. The times are simulated.
32 devices in a mesh: tile: 16 (over z, x, core), member: 2 (over y).
Axes of the slice: x: 2, y: 2, z: 4, core: 2. Of those that a mesh axis runs over, the one named last changes fastest.
Arguments:
- tracers: float32 [4, 12, 4, 192, 256], P('member', None, None, 'tile'), may hold values from -4 to 4
- hydro: float32 [15, 192, 256], P(None, 'tile', 'member'), may hold values from -6 to 6, as said below
- wet: int32 [192, 256], P('tile'), may hold values from 0 to 1, as said below
- rates: float32 [4, 12, 12], P('member'), may hold values from -1.75 to 1.75
- decays: float32 [4, 12], P('member'), may hold values from 0.1 to 2
Outputs:
- final: float32 [4, 12, 4, 192, 256], P('member', None, None, 'tile')
Inputs may be any that keep to these rules, and one draw needn't show every extreme that they name: The wet mask is 0 or 1. `hydro`: planes 8 to 14 lie within -3 to 3.
All inputs are finite; a program needn't handle non-finite values.
Results may differ from a plain program's by a relative error of at most 0.0001.
Values sent between devices are 32-bit elements; how exact they have to be, the bound alone decides.
A program may use at most 128 MiB of HBM per device.

v0:
```python
import jax
import jax.numpy as jnp
from jax import lax
from jax.sharding import PartitionSpec as P

STEPS = 2


def with_halo(block, sides, width):
    for axis, dim in sides:
        count = lax.axis_size(axis)
        forward = [(i, i + 1) for i in range(count - 1)]
        backward = [(target, source) for source, target in forward]
        low = lax.ppermute(
            lax.slice_in_dim(block, block.shape[dim] - width, None, axis=dim), axis, forward
        )
        high = lax.ppermute(lax.slice_in_dim(block, 0, width, axis=dim), axis, backward)
        block = jnp.concatenate([low, block, high], axis=dim)
    return block


def advance(conc, fields, rate, decay):
    inner = conc[..., 2:-2, :]
    padded = jnp.pad(inner, ((0, 0), (0, 0), (0, 0), (0, 0), (2, 2)))
    width = inner.shape[-1]
    east1 = padded[..., 3 : width + 3]
    west1 = padded[..., 1 : width + 1]
    east2 = padded[..., 4 : width + 4]
    west2 = padded[..., 0:width]
    rows = conc.shape[3]
    south1 = conc[..., 3 : rows - 1, :]
    north1 = conc[..., 1 : rows - 3, :]
    south2 = conc[..., 4:, :]
    north2 = conc[..., : rows - 4, :]
    deriv_x = (8.0 * (east1 - west1) - (east2 - west2)) / 12.0
    deriv_y = (8.0 * (south1 - north1) - (south2 - north2)) / 12.0
    lapl = south1 + north1 + east1 + west1 - 4.0 * inner
    vel_x = 0.5 * fields[0:4]
    vel_y = 0.5 * fields[4:8]
    kappa = 0.1 * jnp.exp(0.7 * fields[8:12])
    mixing = 0.05 * jnp.exp(0.7 * fields[12:15])
    mask = fields[15]
    flux = mixing * (inner[:, :, 1:] - inner[:, :, :-1])
    zero_plane = jnp.zeros_like(flux[:, :, :1])
    vert = jnp.concatenate([flux, zero_plane], axis=2) - jnp.concatenate([zero_plane, flux], axis=2)
    react = jnp.einsum("mst,mtlrc->mslrc", rate, jnp.tanh(inner), precision=lax.Precision.HIGHEST)
    react = react - decay[:, :, None, None, None] * inner
    tend = -vel_x * deriv_x - vel_y * deriv_y + kappa * lapl + vert + react
    return mask * (inner + 0.2 * tend)


def on_device(tracers, hydro, wet, rates, decays):
    full_hydro = lax.all_gather(hydro, "member", axis=2, tiled=True)
    fields = jnp.concatenate([full_hydro, wet.astype(jnp.float32)[None]], axis=0)
    conc = tracers
    for step in range(STEPS):
        extended = with_halo(conc, (("tile", 3),), 2)
        conc = advance(extended, fields, rates, decays)
    return conc


def solution(mesh):
    placed = (
        P("member", None, None, "tile", None),
        P(None, "tile", "member"),
        P("tile", None),
        P("member", None, None),
        P("member", None),
    )
    return jax.shard_map(
        on_device,
        mesh=mesh,
        in_specs=placed,
        out_specs=P("member", None, None, "tile", None),
        check_vma=False,
    )
```

profile of v0, /device:TPU:1, one launch (start us, length us, event | category | flops | bytes accessed | tf_op | source)
XLA Modules:
  0.0 35.6 jit_solution(9832506346284676127)
XLA Ops:
  0.0 0.0 copy-start
  0.0 2.1 %copy.36 = f32[2,12,4,12,256]{4,1,3,2,0:T(8,128)S(1)} copy(f32[2,12,4,12,256]{4,2,3,1,0:T(4,128)} %param.5) | data formatting | bytes 2359296 | tf_op args[0]
  2.1 0.0 copy-start.1
  2.1 4.5 %collective-permute-start.1 = (f32[2,12,4,2,256]{4,1,3,2,0:T(8,128)S(1)}, f32[2,12,4,2,256]{4,1,3,2,0:T(8,128)S(1)}, u32[]{:S(2)}, u32[]{:S(2)}) collective-permute-start(f32[2,12,4,2,256]{4,1,3,2,0:T(8,128)S(1)} %get-tuple-element.8), channel_id=1, source_target_pairs={{0,2},{2,4},{4,6},{6,8},{8,10},{10,12},{12,14},{14,16},{16,18},{18... | collective-permute-start | bytes 589832 | tf_op jit(solution)/shard_map/ppermute | solution.py:14
  6.6 1.9 %collective-permute-start = (f32[2,12,4,2,256]{4,1,3,2,0:T(8,128)S(1)}, f32[2,12,4,2,256]{4,1,3,2,0:T(8,128)S(1)}, u32[]{:S(2)}, u32[]{:S(2)}) collective-permute-start(f32[2,12,4,2,256]{4,1,3,2,0:T(8,128)S(1)} %get-tuple-element.7), channel_id=1, source_target_pairs={{2,0},{4,2},{6,4},{8,6},{10,8},{12,10},{14,12},{16,14},{18,16},{20... | collective-permute-start | bytes 589832 | tf_op jit(solution)/shard_map/ppermute | solution.py:17
  8.6 0.0 copy-done
  8.6 0.3 tanh.6
  8.9 0.0 copy-done.1
  8.9 4.4 %all_gather.3 = f32[15,12,256]{2,1,0:T(8,128)S(1)} all-gather(f32[15,12,128]{2,1,0:T(8,128)S(1)} %copy.25), channel_id=1, replica_groups=mesh['tile'=16,'member'=2] {'member'}, dimensions={2}, use_global_device_ids=true | all-gather | bytes 276480 | tf_op jit(solution)/shard_map/all_gather | solution.py:53
  13.4 0.0 copy-start.2
  13.4 0.2 fusion.34
  13.6 0.5 %copy-done.2 = s32[12,256]{1,0:T(8,128)S(1)} copy-done((s32[12,256]{1,0:T(8,128)S(1)}, s32[12,256]{1,0:T(8,128)}, u32[]{:S(2)}) %copy-start.2) | copy-done | bytes 12312
  14.1 0.0 collective-permute-done.1
  14.2 0.0 copy-start.3
  14.2 0.0 copy-start.4
  14.2 0.7 %copy_dynamic-update-slice_fusion.1 = (f32[2,12,4,14,256]{4,1,3,2,0:T(8,128)S(1)}, f32[2,12,4,14,256]{4,1,3,2,0:T(8,128)S(1)}) fusion(f32[2,12,4,12,256]{4,2,3,1,0:T(4,128)S(1)} %copy-done, f32[2,12,4,14,256]{4,1,3,2,0:T(8,128)S(1)} %constant_dynamic-update-slice_fusion.1), kind=kLoop, calls=%fused_computation.52 | loop fusion | bytes 4325376
  14.9 0.0 collective-permute-done
  15.0 0.0 copy-done.3
  15.0 0.0 copy-done.4
  15.0 3.6 %fusion.11 = f32[2,12,4,12,256]{4,1,3,2,0:T(8,128)S(1)} fusion(f32[2,12,4,12,256]{4,1,3,2,0:T(8,128)S(1)} %copy.36, f32[2,12,4,14,256]{4,1,3,2,0:T(8,128)S(1)} %get-tuple-element.10, f32[2,12,4,14,256]{4,1,3,2,0:T(8,128)S(1)} %constant_dynamic-update-slice_fusion, f32[2,12,3,12,256]{4,1,3,2,0:T(8,128)S(1)} %fusion.34, f32[2,12,4,12,256]{4,2,3,1,0:T(4,128)S(1)} %tanh.6, ...), kind=kOutput, calls=%fused_computation.23 | convolution fusion | flops 50135040 | bytes 9303264 | tf_op jit(solution)/shard_map/mst,mtlrc->mslrc/dot_general | solution.py:46
  18.6 1.9 %collective-permute-start.2 = (f32[2,12,4,2,256]{4,1,3,2,0:T(8,128)S(1)}, f32[2,12,4,2,256]{4,1,3,2,0:T(8,128)S(1)}, u32[]{:S(2)}, u32[]{:S(2)}) collective-permute-start(f32[2,12,4,2,256]{4,1,3,2,0:T(8,128)S(1)} %get-tuple-element.5), channel_id=1, source_target_pairs={{2,0},{4,2},{6,4},{8,6},{10,8},{12,10},{14,12},{16,14},{18,16},{20... | collective-permute-start | bytes 589832 | tf_op jit(solution)/shard_map/ppermute | solution.py:17
  20.5 5.1 %collective-permute-start.3 = (f32[2,12,4,2,256]{4,1,3,2,0:T(8,128)S(1)}, f32[2,12,4,2,256]{4,1,3,2,0:T(8,128)S(1)}, u32[]{:S(2)}, u32[]{:S(2)}) collective-permute-start(f32[2,12,4,2,256]{4,1,3,2,0:T(8,128)S(1)} %get-tuple-element.6), channel_id=1, source_target_pairs={{0,2},{2,4},{4,6},{6,8},{8,10},{10,12},{12,14},{14,16},{16,18},{18... | collective-permute-start | bytes 589832 | tf_op jit(solution)/shard_map/ppermute | solution.py:14
  25.6 0.3 fusion.33
  25.9 1.8 %collective-permute-done.2 = f32[2,12,4,2,256]{4,1,3,2,0:T(8,128)S(1)} collective-permute-done((f32[2,12,4,2,256]{4,1,3,2,0:T(8,128)S(1)}, f32[2,12,4,2,256]{4,1,3,2,0:T(8,128)S(1)}, u32[]{:S(2)}, u32[]{:S(2)}) %collective-permute-start.2) | collective-permute-done | bytes 196640 | tf_op jit(solution)/shard_map/ppermute | solution.py:17
  27.7 2.8 %collective-permute-done.3 = f32[2,12,4,2,256]{4,1,3,2,0:T(8,128)S(1)} collective-permute-done((f32[2,12,4,2,256]{4,1,3,2,0:T(8,128)S(1)}, f32[2,12,4,2,256]{4,1,3,2,0:T(8,128)S(1)}, u32[]{:S(2)}, u32[]{:S(2)}) %collective-permute-start.3) | collective-permute-done | bytes 196640 | tf_op jit(solution)/shard_map/ppermute | solution.py:14
  30.5 3.3 %fusion.21 = f32[2,12,4,12,256]{4,1,3,2,0:T(8,128)S(1)} fusion(f32[2,12,4,12,256]{4,1,3,2,0:T(8,128)S(1)} %fusion.11, f32[2,12,4,2,256]{4,1,3,2,0:T(8,128)S(1)} %collective-permute-done.3, f32[2,12,4,2,256]{4,1,3,2,0:T(8,128)S(1)} %collective-permute-done.2, f32[2,12,3,12,256]{4,1,3,2,0:T(8,128)S(1)} %fusion.33, f32[2,12]{1,0:T(2,128)S(1)} %copy-done.4, ...), kind=kOutput, calls=%fused_computation.33 | convolution fusion | flops 51314688 | bytes 6255616 | tf_op jit(solution)/shard_map/mst,mtlrc->mslrc/dot_general | solution.py:46
  33.9 1.8 %copy.38 = f32[2,12,4,12,256]{4,2,3,1,0:T(4,128)} copy(f32[2,12,4,12,256]{4,1,3,2,0:T(8,128)S(1)} %fusion.21) | data formatting | bytes 2359296 | tf_op jit(solution)/shard_map/mul | solution.py:49
  (8 shorter events, 0.2 us)
Async XLA Ops:
  0.0 8.6 %copy-start = (f32[2,12,4,12,256]{4,2,3,1,0:T(4,128)S(1)}, f32[2,12,4,12,256]{4,2,3,1,0:T(4,128)}, u32[]{:S(2)}) copy-start(f32[2,12,4,12,256]{4,2,3,1,0:T(4,128)} %param.5) | copy-start | bytes 3538948
  2.1 6.8 %copy-start.1 = (f32[15,12,128]{2,0,1:T(8,128)S(1)}, f32[15,12,128]{2,0,1:T(8,128)}, u32[]{:S(2)}) copy-start(f32[15,12,128]{2,0,1:T(8,128)} %param.6) | copy-start | bytes 276484
  2.1 12.0 %collective-permute-start.1 = (f32[2,12,4,2,256]{4,1,3,2,0:T(8,128)S(1)}, f32[2,12,4,2,256]{4,1,3,2,0:T(8,128)S(1)}, u32[]{:S(2)}, u32[]{:S(2)}) collective-permute-start(f32[2,12,4,2,256]{4,1,3,2,0:T(8,128)S(1)} %get-tuple-element.8), channel_id=1, source_target_pairs={{0,2},{2,4},{4,6},{6,8},{8,10},{10,12},{12,14},{14,16},{16,18},{18... | collective-permute-start | bytes 589832 | tf_op jit(solution)/shard_map/ppermute | solution.py:14
  6.6 8.3 %collective-permute-start = (f32[2,12,4,2,256]{4,1,3,2,0:T(8,128)S(1)}, f32[2,12,4,2,256]{4,1,3,2,0:T(8,128)S(1)}, u32[]{:S(2)}, u32[]{:S(2)}) collective-permute-start(f32[2,12,4,2,256]{4,1,3,2,0:T(8,128)S(1)} %get-tuple-element.7), channel_id=1, source_target_pairs={{2,0},{4,2},{6,4},{8,6},{10,8},{12,10},{14,12},{16,14},{18,16},{20... | collective-permute-start | bytes 589832 | tf_op jit(solution)/shard_map/ppermute | solution.py:17
  13.4 0.7 %copy-start.2 = (s32[12,256]{1,0:T(8,128)S(1)}, s32[12,256]{1,0:T(8,128)}, u32[]{:S(2)}) copy-start(s32[12,256]{1,0:T(8,128)} %param.7) | copy-start | bytes 36868
  14.2 0.8 %copy-start.3 = (f32[2,12,12]{2,0,1:T(2,128)S(1)}, f32[2,12,12]{2,0,1:T(2,128)}, u32[]{:S(2)}) copy-start(f32[2,12,12]{2,0,1:T(2,128)} %param.8) | copy-start | bytes 3460
  14.2 0.8 %copy-start.4 = (f32[2,12]{1,0:T(2,128)S(1)}, f32[2,12]{1,0:T(2,128)}, u32[]{:S(2)}) copy-start(f32[2,12]{1,0:T(2,128)} %param.9) | copy-start | bytes 292
  18.6 9.1 %collective-permute-start.2 = (f32[2,12,4,2,256]{4,1,3,2,0:T(8,128)S(1)}, f32[2,12,4,2,256]{4,1,3,2,0:T(8,128)S(1)}, u32[]{:S(2)}, u32[]{:S(2)}) collective-permute-start(f32[2,12,4,2,256]{4,1,3,2,0:T(8,128)S(1)} %get-tuple-element.5), channel_id=1, source_target_pairs={{2,0},{4,2},{6,4},{8,6},{10,8},{12,10},{14,12},{16,14},{18,16},{20... | collective-permute-start | bytes 589832 | tf_op jit(solution)/shard_map/ppermute | solution.py:17
  20.5 10.0 %collective-permute-start.3 = (f32[2,12,4,2,256]{4,1,3,2,0:T(8,128)S(1)}, f32[2,12,4,2,256]{4,1,3,2,0:T(8,128)S(1)}, u32[]{:S(2)}, u32[]{:S(2)}) collective-permute-start(f32[2,12,4,2,256]{4,1,3,2,0:T(8,128)S(1)} %get-tuple-element.6), channel_id=1, source_target_pairs={{0,2},{2,4},{4,6},{6,8},{8,10},{10,12},{12,14},{14,16},{16,18},{18... | collective-permute-start | bytes 589832 | tf_op jit(solution)/shard_map/ppermute | solution.py:14
where the time goes:
time: 36 us; the launch traced here: 35.6 us
  starting transfers between devices  13.4 us (37%)
  matrix products  6.9 us (19%)
  local copies, waits for them, and re-layouts  5.54 us (15%)
  waiting for transfers between devices  4.63 us (13%)
  blocking collectives  4.41 us (12%)
  other arithmetic  0.52 us (1%)
    ppermute x2, starting transfers between devices, with_halo(): lax.ppermute(lax.slice_in_dim(block, block.shape[dim] - width, None, axis...  9.58 us
    dot_general x2, matrix products, advance(): jnp.einsum('mst,mtlrc->mslrc', rate, jnp.tanh(inner), precision=lax.Preci...  6.9 us
    all_gather x1, blocking collectives, on_device(): full_hydro = lax.all_gather(hydro, 'member', axis=2, tiled=True)  4.41 us
    ppermute x2, starting transfers between devices, with_halo(): lax.ppermute(lax.slice_in_dim(block, 0, width, axis=dim), axis, backward)  3.84 us
    unnamed x14, local copies, waits for them, and re-layouts  3.35 us
    ppermute x2, waiting for transfers between devices, with_halo(): lax.ppermute(lax.slice_in_dim(block, block.shape[dim] - width, None, axis...  2.8 us
    ppermute x2, waiting for transfers between devices, with_halo(): lax.ppermute(lax.slice_in_dim(block, 0, width, axis=dim), axis, backward)  1.83 us
    mul x1, local copies, waits for them, and re-layouts, advance(): return mask * (inner + 0.2 * tend)  1.77 us
  transfers between devices with their start and end apart: 4, of which 2 were waited for; matrix products, arithmetic and copies ran while one was open for 4% of the time, Pallas kernels for 0%

commit v1 on v0

v1 whole, which is shorter than its diff:
```python
import functools

import jax
import jax.numpy as jnp
from jax import lax
from jax.experimental import pallas as pl
from jax.experimental.pallas import tpu as pltpu
from jax.sharding import PartitionSpec as P

SUB, LANE = 8, 128
CHUNK = 4


def kernel(
    members, tiles, tr, hyin, wet, rates, decays, out,
    c0, c1, hy, msk, coef, wmain, wlow, dec,
    load_sem, tr_send, tr_recv, hy_send, hy_recv, up_send, up_recv, dn_send, dn_recv,
    wet_send, wet_recv,
):
    local_m, tracers = rates.shape[0], rates.shape[1]
    rows, pairs = tr.shape[1], tr.shape[2]
    wide = tracers * SUB
    tile = lax.axis_index("tile")
    member = lax.axis_index("member")
    has_up = tile > 0
    has_dn = tile < tiles - 1

    barrier = pltpu.get_barrier_semaphore()

    def greet(where):
        pl.semaphore_signal(barrier, inc=1, device_id=where, device_id_type=pl.DeviceIdType.MESH)

    def other(d):
        return lax.rem(member + d, members)

    for d in range(1, members):
        greet({"tile": tile, "member": other(d)})

    @pl.when(has_up)
    def _():
        for d in range(members):
            greet({"tile": tile - 1, "member": other(d)})

    @pl.when(has_dn)
    def _():
        for d in range(members):
            greet({"tile": tile + 1, "member": other(d)})

    load_tr = pltpu.make_async_copy(tr, c0.at[:, pl.ds(4, rows)], load_sem.at[0])
    load_hy = pltpu.make_async_copy(hyin, hy.at[member, pl.ds(2, rows)], load_sem.at[1])
    load_tr.start()
    load_hy.start()

    sub = lax.broadcasted_iota(jnp.int32, (SUB, LANE), 0)
    lane = lax.broadcasted_iota(jnp.int32, (SUB, LANE), 1)
    left = sub < 4
    for r in range(rows):
        for p in range(pairs):
            a = jnp.broadcast_to(wet[r : r + 1, 2 * p * LANE : (2 * p + 1) * LANE], (SUB, LANE))
            b = jnp.broadcast_to(wet[r : r + 1, (2 * p + 1) * LANE : (2 * p + 2) * LANE], (SUB, LANE))
            msk[r + 2, p] = jnp.where(left, a, b).astype(jnp.float32)

    def remote(src, dst, send, recv, where):
        return pltpu.make_async_remote_copy(
            src_ref=src, dst_ref=dst, send_sem=send, recv_sem=recv,
            device_id=where, device_id_type=pl.DeviceIdType.MESH,
        )

    def tr_copy(k):
        source, target = ((0, rows + 4), (rows - 2, 2), (2, rows + 6), (rows - 4, 0))[k]
        step = -1 if k % 2 == 0 else 1
        return remote(
            tr.at[:, pl.ds(source, 2)], c0.at[:, pl.ds(target, 2)], tr_send.at[k], tr_recv.at[k],
            {"tile": tile + step, "member": member},
        )

    def hy_copy(d, slot):
        return remote(
            hyin, hy.at[slot, pl.ds(2, rows)], hy_send.at[d - 1], hy_recv.at[d - 1],
            {"tile": tile, "member": other(d)},
        )

    def up_copy(d, slot):
        return remote(
            hyin.at[pl.ds(0, 2)], hy.at[slot, pl.ds(rows + 2, 2)], up_send.at[d], up_recv.at[d],
            {"tile": tile - 1, "member": other(d)},
        )

    def dn_copy(d, slot):
        return remote(
            hyin.at[pl.ds(rows - 2, 2)], hy.at[slot, pl.ds(0, 2)], dn_send.at[d], dn_recv.at[d],
            {"tile": tile + 1, "member": other(d)},
        )

    def wet_copy(k):
        source, target = ((2, rows + 2), (rows, 0))[k]
        step = -1 if k == 0 else 1
        return remote(
            msk.at[pl.ds(source, 2)], msk.at[pl.ds(target, 2)], wet_send.at[k], wet_recv.at[k],
            {"tile": tile + step, "member": member},
        )

    partners = members - 1 + members * (has_up.astype(jnp.int32) + has_dn.astype(jnp.int32))
    pl.semaphore_wait(barrier, partners)

    for d in range(1, members):
        hy_copy(d, member).start()

    @pl.when(has_up)
    def _():
        tr_copy(0).start()
        for d in range(members):
            up_copy(d, member).start()
        wet_copy(0).start()
        tr_copy(2).start()

    @pl.when(has_dn)
    def _():
        tr_copy(1).start()
        for d in range(members):
            dn_copy(d, member).start()
        wet_copy(1).start()
        tr_copy(3).start()

    @pl.when(jnp.logical_not(has_up))
    def _():
        c0[:, 0:4] = jnp.zeros_like(c0[:, 0:4])
        hy[:, 0:2] = jnp.zeros_like(hy[:, 0:2])
        msk[0:2] = jnp.zeros_like(msk[0:2])

    @pl.when(jnp.logical_not(has_dn))
    def _():
        c0[:, rows + 4 :] = jnp.zeros_like(c0[:, rows + 4 :])
        hy[:, rows + 2 :] = jnp.zeros_like(hy[:, rows + 2 :])
        msk[rows + 2 :] = jnp.zeros_like(msk[rows + 2 :])

    for m in range(local_m):
        spread = jnp.broadcast_to(rates[m][:, None, :], (tracers, SUB, tracers)).reshape(wide, tracers)
        row_t = lax.broadcasted_iota(jnp.int32, (tracers, 2 * wide), 0)
        col_t = lax.broadcasted_iota(jnp.int32, (tracers, 2 * wide), 1)
        pick = (lax.rem(col_t, wide) // SUB == row_t).astype(jnp.float32)
        full = jnp.dot(spread, pick, precision=lax.Precision.HIGHEST, preferred_element_type=jnp.float32)
        row_a = lax.broadcasted_iota(jnp.int32, (wide, 2 * wide), 0)
        col_a = lax.broadcasted_iota(jnp.int32, (wide, 2 * wide), 1)
        full = jnp.where(lax.rem(row_a, SUB) == lax.rem(col_a, SUB), full, 0.0)
        high = full.astype(jnp.bfloat16)
        wmain[m] = high
        wlow[m] = (full - high.astype(jnp.float32)).astype(jnp.bfloat16)[:, :wide]
        row_d = lax.broadcasted_iota(jnp.int32, (wide, tracers), 0)
        col_d = lax.broadcasted_iota(jnp.int32, (wide, tracers), 1)
        loss = jnp.where(row_d // SUB == col_d, jnp.broadcast_to(decays[m : m + 1, :], (wide, tracers)), 0.0)
        loss = jnp.broadcast_to(jnp.sum(loss, axis=1, keepdims=True), (wide, LANE))
        dec[m * tracers : (m + 1) * tracers] = loss.reshape(tracers, SUB, LANE)

    inner_layer = lax.rem(sub, 4) != 3

    def coefficients(start, stride, count):
        def body(k, carry):
            r = start + stride * k + 2
            for p in range(pairs):
                pad = jnp.zeros((1, LANE), jnp.float32)
                a0 = hy[2 * p, r, 0:8]
                b0 = hy[2 * p + 1, r, 0:8]
                a1 = jnp.concatenate([hy[2 * p, r, 8:15], pad], axis=0)
                b1 = jnp.concatenate([hy[2 * p + 1, r, 8:15], pad], axis=0)
                u = 0.5 * jnp.where(left, a0, pltpu.roll(b0, 4, 0))
                v = 0.5 * jnp.where(left, pltpu.roll(a0, 4, 0), b0)
                kappa = 0.1 * jnp.exp(0.7 * jnp.where(left, a1, pltpu.roll(b1, 4, 0)))
                kz = 0.05 * jnp.exp(0.7 * jnp.where(left, pltpu.roll(a1, 4, 0), b1))
                kz = jnp.where(inner_layer, kz, 0.0)
                mask = msk[r, p]
                s = 0.2 * mask
                kk = s * kappa
                up = s * kz
                down = s * pltpu.roll(kz, 1, 0)
                su, sv = s * u, s * v
                coef[r, p, 0] = mask - 4.0 * kk - up - down
                coef[r, p, 1] = kk - su * (8.0 / 12.0)
                coef[r, p, 2] = kk + su * (8.0 / 12.0)
                coef[r, p, 3] = su * (1.0 / 12.0)
                coef[r, p, 4] = kk - sv * (8.0 / 12.0)
                coef[r, p, 5] = kk + sv * (8.0 / 12.0)
                coef[r, p, 6] = sv * (1.0 / 12.0)
                coef[r, p, 7] = up
                coef[r, p, 8] = down
                coef[r, p, 9] = s
            return carry

        lax.fori_loop(0, count, body, 0)

    def advance(src, src_off, dst, dst_off, start, stride, count):
        def body(k, carry):
            first = start + stride * k
            for p in range(pairs):
                react = []
                for m in range(local_m):
                    part = [
                        jnp.tanh(src[m * tracers : (m + 1) * tracers, first + src_off + j, p]).reshape(wide, LANE)
                        for j in range(2)
                    ]
                    part = jnp.concatenate(part, axis=1)
                    high = part.astype(jnp.bfloat16)
                    low = (part - high.astype(jnp.float32)).astype(jnp.bfloat16)
                    both = jnp.concatenate([high, low], axis=0)
                    react.append(
                        jnp.dot(wmain[m], both, preferred_element_type=jnp.float32)
                        + jnp.dot(wlow[m], high, preferred_element_type=jnp.float32)
                    )
                for j in range(2):
                    r = first + j
                    q = r + src_off
                    k0, ke, kw, kx, ks, kn, ky, ku, kd, s = (coef[r + 2, p, i] for i in range(10))
                    for m in range(local_m):
                        mine = react[m][:, j * LANE : (j + 1) * LANE].reshape(tracers, SUB, LANE)
                        for t in range(0, tracers, CHUNK):
                            g = slice(m * tracers + t, m * tracers + t + CHUNK)
                            c = src[g, q, p]
                            swap = pltpu.roll(c, 4, 1)
                            east = pltpu.roll(src[g, q, p + 1], 4, 1) if p + 1 < pairs else 0.0
                            west = pltpu.roll(src[g, q, p - 1], 4, 1) if p > 0 else 0.0
                            xe = jnp.where(left, swap, east)
                            xw = jnp.where(left, west, swap)
                            e1 = pltpu.roll(jnp.where(lane < 1, xe, c), LANE - 1, 2)
                            e2 = pltpu.roll(jnp.where(lane < 2, xe, c), LANE - 2, 2)
                            w1 = pltpu.roll(jnp.where(lane >= LANE - 1, xw, c), 1, 2)
                            w2 = pltpu.roll(jnp.where(lane >= LANE - 2, xw, c), 2, 2)
                            total = k0 * c + s * (mine[t : t + CHUNK] - dec[g] * c)
                            total += ke * e1 + kw * w1 + kx * (e2 - w2)
                            total += ks * src[g, q + 1, p] + kn * src[g, q - 1, p]
                            total += ky * (src[g, q + 2, p] - src[g, q - 2, p])
                            total += ku * pltpu.roll(c, SUB - 1, 1) + kd * pltpu.roll(c, 1, 1)
                            dst[g, r + dst_off, p] = total
            return carry

        lax.fori_loop(0, count, body, 0)

    load_hy.wait()
    for d in range(1, members):
        hy_copy(d, lax.rem(member + members - d, members)).wait_recv()
    coefficients(0, 1, rows)
    load_tr.wait()
    advance(c0, 4, c1, 2, 2, 2, (rows - 4) // 2)

    @pl.when(has_dn)
    def _():
        tr_copy(0).wait_recv()

    @pl.when(has_up)
    def _():
        tr_copy(1).wait_recv()

    advance(c0, 4, c1, 2, 0, rows - 2, 2)
    advance(c1, 2, out, 0, 2, 2, (rows - 4) // 2)

    @pl.when(has_dn)
    def _():
        for d in range(members):
            up_copy(d, lax.rem(member + members - d, members)).wait_recv()
        wet_copy(0).wait_recv()
        tr_copy(2).wait_recv()

    @pl.when(has_up)
    def _():
        for d in range(members):
            dn_copy(d, lax.rem(member + members - d, members)).wait_recv()
        wet_copy(1).wait_recv()
        tr_copy(3).wait_recv()

    coefficients(-2, 1, 2)
    coefficients(rows, 1, 2)
    advance(c0, 4, c1, 2, -2, rows + 2, 2)
    advance(c1, 2, out, 0, 0, rows - 2, 2)

    for d in range(1, members):
        hy_copy(d, member).wait_send()

    @pl.when(has_up)
    def _():
        for d in range(members):
            up_copy(d, member).wait_send()
        for k in (0, 2):
            tr_copy(k).wait_send()
        wet_copy(0).wait_send()

    @pl.when(has_dn)
    def _():
        for d in range(members):
            dn_copy(d, member).wait_send()
        for k in (1, 3):
            tr_copy(k).wait_send()
        wet_copy(1).wait_send()


def on_device(members, tiles, tracers, hydro, wet, rates, decays):
    local_m, count, layers, rows, cols = tracers.shape
    tiles_c = cols // LANE
    pairs = tiles_c // 2
    groups = local_m * count
    conc = tracers.transpose(0, 1, 3, 2, 4).reshape(local_m, count, rows, layers, tiles_c, LANE)
    conc = conc.transpose(0, 1, 2, 4, 3, 5).reshape(groups, rows, pairs, SUB, LANE)
    planes = hydro.transpose(1, 0, 2)
    dma = pltpu.SemaphoreType.DMA
    wide = count * SUB
    vmem = pl.BlockSpec(memory_space=pltpu.VMEM)
    anywhere = pl.BlockSpec(memory_space=pl.ANY)
    result = pl.pallas_call(
        functools.partial(kernel, members, tiles),
        out_shape=jax.ShapeDtypeStruct(conc.shape, jnp.float32),
        in_specs=[anywhere, anywhere, vmem, vmem, vmem],
        out_specs=vmem,
        scratch_shapes=[
            pltpu.VMEM((groups, rows + 8, pairs, SUB, LANE), jnp.float32),
            pltpu.VMEM((groups, rows + 4, pairs, SUB, LANE), jnp.float32),
            pltpu.VMEM((members, rows + 4, planes.shape[1], LANE), jnp.float32),
            pltpu.VMEM((rows + 4, pairs, SUB, LANE), jnp.float32),
            pltpu.VMEM((rows + 4, pairs, 10, SUB, LANE), jnp.float32),
            pltpu.VMEM((local_m, wide, 2 * wide), jnp.bfloat16),
            pltpu.VMEM((local_m, wide, wide), jnp.bfloat16),
            pltpu.VMEM((groups, SUB, LANE), jnp.float32),
            dma((2,)),
            dma((4,)), dma((4,)),
            dma((max(members - 1, 1),)), dma((max(members - 1, 1),)),
            dma((members,)), dma((members,)),
            dma((members,)), dma((members,)),
            dma((2,)), dma((2,)),
        ],
        compiler_params=pltpu.CompilerParams(
            collective_id=0, has_side_effects=True, vmem_limit_bytes=48 * 1024 * 1024
        ),
    )(conc, planes, wet, rates, decays)
    result = result.reshape(local_m, count, rows, tiles_c, layers, LANE).transpose(0, 1, 2, 4, 3, 5)
    return result.reshape(local_m, count, rows, layers, cols).transpose(0, 1, 3, 2, 4)


def solution(mesh):
    placed = (
        P("member", None, None, "tile", None),
        P(None, "tile", "member"),
        P("tile", None),
        P("member", None, None),
        P("member", None),
    )
    return jax.shard_map(
        functools.partial(on_device, mesh.shape["member"], mesh.shape["tile"]),
        mesh=mesh,
        in_specs=placed,
        out_specs=P("member", None, None, "tile", None),
        check_vma=False,
    )
```

time: 36 us -> 21.1 us (0.59)
  the two profiles are of different devices: /device:TPU:1 before, /device:TPU:17 now
where the time goes in v1:
time: 21.1 us; the launch traced here: 20.8 us
  Pallas kernels  15.5 us (73%)
  local copies, waits for them, and re-layouts  5.28 us (25%)
    pallas_call x1, Pallas kernels, on_device(): pl.pallas_call(functools.partial(kernel, members, tiles), out_shape=jax.S...  15.5 us
    unnamed x10, local copies, waits for them, and re-layouts  5.28 us

profile of v1, /device:TPU:17, one launch (start us, length us, event | category | flops | bytes accessed | tf_op | source)
XLA Modules:
  0.0 20.8 jit_solution(1815902084301841300)
XLA Ops:
  0.0 0.7 %copy.7.rates = f32[2,12,12]{2,1,0:T(8,128)S(1)} copy(f32[2,12,12]{2,0,1:T(2,128)} %param.8) | data formatting | bytes 2304 | tf_op args[3]
  0.7 0.0 copy-start
  0.7 1.3 %copy-done = f32[2,12,4,12,256]{4,2,3,1,0:T(4,128)S(1)} copy-done((f32[2,12,4,12,256]{4,2,3,1,0:T(4,128)S(1)}, f32[2,12,4,12,256]{4,2,3,1,0:T(4,128)}, u32[]{:S(2)}) %copy-start) | copy-done | bytes 1179672
  2.0 0.0 copy-start.1
  2.0 0.9 %copy-done.1 = f32[15,12,128]{2,0,1:T(8,128)S(1)} copy-done((f32[15,12,128]{2,0,1:T(8,128)S(1)}, f32[15,12,128]{2,0,1:T(8,128)}, u32[]{:S(2)}) %copy-start.1) | copy-done | bytes 92184
  2.9 0.0 copy-start.2
  2.9 0.7 %copy-done.2 = s32[12,256]{1,0:T(8,128)S(1)} copy-done((s32[12,256]{1,0:T(8,128)S(1)}, s32[12,256]{1,0:T(8,128)}, u32[]{:S(2)}) %copy-start.2) | copy-done | bytes 12312
  3.6 0.0 copy-start.3
  3.6 0.7 %copy-done.3 = f32[2,12]{1,0:T(2,128)S(1)} copy-done((f32[2,12]{1,0:T(2,128)S(1)}, f32[2,12]{1,0:T(2,128)}, u32[]{:S(2)}) %copy-start.3) | copy-done | bytes 120
  4.3 15.5 %shard_map.55 = f32[24,12,1,8,128]{4,3,2,1,0:T(8,128)S(1)} custom-call(f32[24,12,1,8,128]{4,3,2,1,0:T(8,128)S(1)} %bitcast.16, f32[12,15,128]{2,1,0:T(8,128)S(1)} %bitcast.17, s32[12,256]{1,0:T(8,128)S(1)} %copy-done.2, f32[2,12,12]{2,1,0:T(8,128)S(1)} %copy.7.rates, f32[2,12]{1,0:T(2,128)S(1)} %copy-done.3), custom_call_target="tpu_custom_call" | custom-call | tf_op jit(solution)/shard_map/pallas_call | solution.py:306
  19.8 1.0 %copy.9 = f32[2,12,4,12,256]{4,2,3,1,0:T(4,128)} copy(f32[2,12,4,12,256]{4,2,3,1,0:T(4,128)S(1)} %bitcast.15) | data formatting | bytes 2359296
Async XLA Ops:
  0.7 1.3 %copy-start = (f32[2,12,4,12,256]{4,2,3,1,0:T(4,128)S(1)}, f32[2,12,4,12,256]{4,2,3,1,0:T(4,128)}, u32[]{:S(2)}) copy-start(f32[2,12,4,12,256]{4,2,3,1,0:T(4,128)} %param.5) | copy-start | bytes 3538948
  2.0 0.9 %copy-start.1 = (f32[15,12,128]{2,0,1:T(8,128)S(1)}, f32[15,12,128]{2,0,1:T(8,128)}, u32[]{:S(2)}) copy-start(f32[15,12,128]{2,0,1:T(8,128)} %param.6) | copy-start | bytes 276484
  2.9 0.7 %copy-start.2 = (s32[12,256]{1,0:T(8,128)S(1)}, s32[12,256]{1,0:T(8,128)}, u32[]{:S(2)}) copy-start(s32[12,256]{1,0:T(8,128)} %wet.1) | copy-start | bytes 36868
  3.6 0.7 %copy-start.3 = (f32[2,12]{1,0:T(2,128)S(1)}, f32[2,12]{1,0:T(2,128)}, u32[]{:S(2)}) copy-start(f32[2,12]{1,0:T(2,128)} %decays.1) | copy-start | bytes 292

commit v2 on v1

v2 whole, which is shorter than its diff:
```python
import functools

import jax
import jax.numpy as jnp
from jax import lax
from jax.experimental import pallas as pl
from jax.experimental.pallas import tpu as pltpu
from jax.sharding import PartitionSpec as P

SUB, LANE = 8, 128
CHUNK = 4


def kernel(
    members, tiles, tr, hyin, wet_in, rates_in, decays_in, out,
    c0, c1, hy, wet, rates, decays, stage, hx, msk, coef, wmain, wlow, dec,
    load_sem, slow_send, slow_recv, fast_send, fast_recv, hy_send, hy_recv,
    stage_send, stage_recv, relay_send, relay_recv,
):
    tracers, local_m = rates.shape[0], rates.shape[1]
    rows, pairs = tr.shape[1], tr.shape[2]
    wide = tracers * SUB
    tile = lax.axis_index("tile")
    member = lax.axis_index("member")
    odd = lax.rem(tile, 2)
    slow_tile = tile - 1 + 2 * odd
    fast_tile = tile + 1 - 2 * odd
    has_slow = jnp.logical_and(slow_tile >= 0, slow_tile < tiles)
    slow_id = {"tile": slow_tile, "member": member}
    fast_id = {"tile": fast_tile, "member": member}

    barrier = pltpu.get_barrier_semaphore()

    def greet(where):
        pl.semaphore_signal(barrier, inc=1, device_id=where, device_id_type=pl.DeviceIdType.MESH)

    def other(d):
        return lax.rem(member + d, members)

    @pl.when(has_slow)
    def _():
        greet(slow_id)

    greet(fast_id)
    for d in range(1, members):
        greet({"tile": tile, "member": other(d)})

    loads = [
        pltpu.make_async_copy(hyin, hy.at[member], load_sem.at[0]),
        pltpu.make_async_copy(wet_in, wet, load_sem.at[1]),
        pltpu.make_async_copy(rates_in, rates, load_sem.at[2]),
        pltpu.make_async_copy(decays_in, decays, load_sem.at[3]),
        pltpu.make_async_copy(tr, c0.at[:, pl.ds(4, rows)], load_sem.at[4]),
    ]
    for load in loads:
        load.start()

    sub = lax.broadcasted_iota(jnp.int32, (SUB, LANE), 0)
    lane = lax.broadcasted_iota(jnp.int32, (SUB, LANE), 1)
    left = sub < 4

    def remote(src, dst, send, recv, where):
        return pltpu.make_async_remote_copy(
            src_ref=src, dst_ref=dst, send_sem=send, recv_sem=recv,
            device_id=where, device_id_type=pl.DeviceIdType.MESH,
        )

    def group(ref, m, row):
        return ref.at[pl.ds(m * tracers, tracers), pl.ds(row, 2)]

    def slow_copy(m, far):
        source = 2 + odd * (rows - 6) if far else odd * (rows - 2)
        target = (1 - odd) * (rows + 6) if far else rows + 4 - odd * (rows + 2)
        k = 2 * m + far
        return remote(group(tr, m, source), group(c0, m, target), slow_send.at[k], slow_recv.at[k], slow_id)

    def slow_arrival(m, far):
        target = odd * (rows + 6) if far else 2 + odd * (rows + 2)
        k = 2 * m + far
        return remote(group(tr, m, 0), group(c0, m, target), slow_send.at[k], slow_recv.at[k], slow_id)

    def fast_copy(m, far):
        source = rows - 4 - odd * (rows - 6) if far else (1 - odd) * (rows - 2)
        target = odd * (rows + 6) if far else 2 + odd * (rows + 2)
        k = 2 * m + far
        return remote(group(tr, m, source), group(c0, m, target), fast_send.at[k], fast_recv.at[k], fast_id)

    def fast_arrival(m, far):
        target = (1 - odd) * (rows + 6) if far else rows + 4 - odd * (rows + 2)
        k = 2 * m + far
        return remote(group(tr, m, 0), group(c0, m, target), fast_send.at[k], fast_recv.at[k], fast_id)

    def hy_copy(d, slot):
        return remote(
            hyin, hy.at[slot], hy_send.at[d - 1], hy_recv.at[d - 1], {"tile": tile, "member": other(d)}
        )

    def stage_copy(side):
        return remote(
            stage.at[side], hx.at[side, member], stage_send.at[side], stage_recv.at[side],
            (slow_id, fast_id)[side],
        )

    def relay_copy(side, d, slot):
        k = side * max(members - 1, 1) + d - 1
        return remote(
            hx.at[side, slot], hx.at[side, slot], relay_send.at[k], relay_recv.at[k],
            {"tile": tile, "member": other(d)},
        )

    pl.semaphore_wait(barrier, members + has_slow.astype(jnp.int32))

    @pl.when(has_slow)
    def _():
        for m in range(local_m):
            for far in range(2):
                slow_copy(m, far).start()

    for d in range(1, members):
        hy_copy(d, member).start()
    for m in range(local_m):
        for far in range(2):
            fast_copy(m, far).start()

    loads[0].wait()
    loads[1].wait()

    def wet_row(r):
        row = wet[r : r + 1, 0:LANE]
        for q in range(1, members):
            row = jnp.where(member == q, wet[r : r + 1, q * LANE : (q + 1) * LANE], row)
        return row.astype(jnp.float32)

    for j in range(2):
        low_row, high_row = wet_row(j), wet_row(rows - 2 + j)
        for side in range(2):
            low_side = odd == side
            first = odd * (rows - 2) if side == 0 else (1 - odd) * (rows - 2)
            stage[side, j, 0:15] = hy[member, first + j]
            stage[side, j, 15:16] = jnp.where(low_side, low_row, high_row)

    @pl.when(has_slow)
    def _():
        stage_copy(0).start()

    stage_copy(1).start()

    @pl.when(jnp.logical_not(has_slow))
    def _():
        c0[:, pl.ds(odd * (rows + 4), 4)] = jnp.zeros((c0.shape[0], 4) + c0.shape[2:], jnp.float32)
        hx[0] = jnp.zeros(hx.shape[1:], jnp.float32)

    loads[2].wait()
    loads[3].wait()

    for m in range(local_m):
        spread = jnp.broadcast_to(rates[:, m][:, None, :], (tracers, SUB, tracers)).reshape(wide, tracers)
        row_t = lax.broadcasted_iota(jnp.int32, (tracers, 2 * wide), 0)
        col_t = lax.broadcasted_iota(jnp.int32, (tracers, 2 * wide), 1)
        pick = (lax.rem(col_t, wide) // SUB == row_t).astype(jnp.float32)
        full = jnp.dot(spread, pick, precision=lax.Precision.HIGHEST, preferred_element_type=jnp.float32)
        row_a = lax.broadcasted_iota(jnp.int32, (wide, 2 * wide), 0)
        col_a = lax.broadcasted_iota(jnp.int32, (wide, 2 * wide), 1)
        full = jnp.where(lax.rem(row_a, SUB) == lax.rem(col_a, SUB), full, 0.0)
        high = full.astype(jnp.bfloat16)
        wmain[m] = high
        wlow[m] = (full - high.astype(jnp.float32)).astype(jnp.bfloat16)[:, :wide]
        row_d = lax.broadcasted_iota(jnp.int32, (wide, tracers), 0)
        col_d = lax.broadcasted_iota(jnp.int32, (wide, tracers), 1)
        loss = jnp.where(row_d // SUB == col_d, jnp.broadcast_to(decays[m : m + 1, :], (wide, tracers)), 0.0)
        loss = jnp.broadcast_to(jnp.sum(loss, axis=1, keepdims=True), (wide, LANE))
        dec[m * tracers : (m + 1) * tracers] = loss.reshape(tracers, SUB, LANE)

    inner_layer = lax.rem(sub, 4) != 3

    def coefficients(r, p, a0, b0, a1, b1, mask):
        u = 0.5 * jnp.where(left, a0, pltpu.roll(b0, 4, 0))
        v = 0.5 * jnp.where(left, pltpu.roll(a0, 4, 0), b0)
        kappa = 0.1 * jnp.exp(0.7 * jnp.where(left, a1, pltpu.roll(b1, 4, 0)))
        kz = 0.05 * jnp.exp(0.7 * jnp.where(left, pltpu.roll(a1, 4, 0), b1))
        kz = jnp.where(inner_layer, kz, 0.0)
        s = 0.2 * mask
        kk = s * kappa
        up = s * kz
        down = s * pltpu.roll(kz, 1, 0)
        su, sv = s * u, s * v
        coef[r, p, 0] = mask - 4.0 * kk - up - down
        coef[r, p, 1] = kk - su * (8.0 / 12.0)
        coef[r, p, 2] = kk + su * (8.0 / 12.0)
        coef[r, p, 3] = su * (1.0 / 12.0)
        coef[r, p, 4] = kk - sv * (8.0 / 12.0)
        coef[r, p, 5] = kk + sv * (8.0 / 12.0)
        coef[r, p, 6] = sv * (1.0 / 12.0)
        coef[r, p, 7] = up
        coef[r, p, 8] = down
        coef[r, p, 9] = s

    for r in range(rows):
        for p in range(pairs):
            a = jnp.broadcast_to(wet[r : r + 1, 2 * p * LANE : (2 * p + 1) * LANE], (SUB, LANE))
            b = jnp.broadcast_to(wet[r : r + 1, (2 * p + 1) * LANE : (2 * p + 2) * LANE], (SUB, LANE))
            msk[r, p] = jnp.where(left, a, b).astype(jnp.float32)

    def own_coefficients():
        def body(r, carry):
            pad = jnp.zeros((1, LANE), jnp.float32)
            for p in range(pairs):
                blocks = []
                for q in (2 * p, 2 * p + 1):
                    blocks.append(hy[q, r, 0:8])
                    blocks.append(jnp.concatenate([hy[q, r, 8:15], pad], axis=0))
                a0, a1, b0, b1 = blocks
                coefficients(r + 2, p, a0, b0, a1, b1, msk[r, p])
            return carry

        lax.fori_loop(0, rows, body, 0)

    def halo_coefficients(side):
        first = odd * (rows + 2) if side == 0 else (1 - odd) * (rows + 2)

        def body(j, carry):
            for p in range(pairs):
                a, b = 2 * p, 2 * p + 1
                mask = jnp.where(
                    left,
                    jnp.broadcast_to(hx[side, a, j, 15:16], (SUB, LANE)),
                    jnp.broadcast_to(hx[side, b, j, 15:16], (SUB, LANE)),
                )
                coefficients(
                    first + j, p, hx[side, a, j, 0:8], hx[side, b, j, 0:8],
                    hx[side, a, j, 8:16], hx[side, b, j, 8:16], mask,
                )
            return carry

        lax.fori_loop(0, 2, body, 0)

    def advance(src, src_off, dst, dst_off, start, stride, count, ms):
        def body(k, carry):
            first = start + stride * k
            for p in range(pairs):
                react = []
                for m in ms:
                    part = [
                        jnp.tanh(src[pl.ds(m * tracers, tracers), first + src_off + j, p]).reshape(wide, LANE)
                        for j in range(2)
                    ]
                    part = jnp.concatenate(part, axis=1)
                    high = part.astype(jnp.bfloat16)
                    low = (part - high.astype(jnp.float32)).astype(jnp.bfloat16)
                    both = jnp.concatenate([high, low], axis=0)
                    react.append(
                        jnp.dot(wmain[m], both, preferred_element_type=jnp.float32)
                        + jnp.dot(wlow[m], high, preferred_element_type=jnp.float32)
                    )
                for j in range(2):
                    r = first + j
                    q = r + src_off
                    k0, ke, kw, kx, ks, kn, ky, ku, kd, s = (coef[r + 2, p, i] for i in range(10))
                    for n, m in enumerate(ms):
                        mine = react[n][:, j * LANE : (j + 1) * LANE].reshape(tracers, SUB, LANE)
                        for t in range(0, tracers, CHUNK):
                            g = pl.ds(m * tracers + t, CHUNK)
                            c = src[g, q, p]
                            swap = pltpu.roll(c, 4, 1)
                            east = pltpu.roll(src[g, q, p + 1], 4, 1) if p + 1 < pairs else 0.0
                            west = pltpu.roll(src[g, q, p - 1], 4, 1) if p > 0 else 0.0
                            xe = jnp.where(left, swap, east)
                            xw = jnp.where(left, west, swap)
                            e1 = pltpu.roll(jnp.where(lane < 1, xe, c), LANE - 1, 2)
                            e2 = pltpu.roll(jnp.where(lane < 2, xe, c), LANE - 2, 2)
                            w1 = pltpu.roll(jnp.where(lane >= LANE - 1, xw, c), 1, 2)
                            w2 = pltpu.roll(jnp.where(lane >= LANE - 2, xw, c), 2, 2)
                            total = k0 * c + s * (mine[t : t + CHUNK] - dec[g] * c)
                            total += ke * e1 + kw * w1 + kx * (e2 - w2)
                            total += ks * src[g, q + 1, p] + kn * src[g, q - 1, p]
                            total += ky * (src[g, q + 2, p] - src[g, q - 2, p])
                            total += ku * pltpu.roll(c, SUB - 1, 1) + kd * pltpu.roll(c, 1, 1)
                            dst[g, r + dst_off, p] = total
            return carry

        if count == 1:
            body(0, 0)
        else:
            lax.fori_loop(0, count, body, 0)

    for d in range(1, members):
        hy_copy(d, lax.rem(member + members - d, members)).wait_recv()
    own_coefficients()
    loads[4].wait()
    every = list(range(local_m))
    advance(c0, 4, c1, 2, 2, 2, (rows - 4) // 2, every)

    def relay(side):
        stage_copy(side).wait_recv()
        for d in range(1, members):
            relay_copy(side, d, member).start()

    relay(1)

    @pl.when(has_slow)
    def _():
        relay(0)

    for m in every:
        for far in range(2):
            fast_arrival(m, far).wait_recv()
    for d in range(1, members):
        relay_copy(1, d, lax.rem(member + members - d, members)).wait_recv()
    halo_coefficients(1)
    advance(c0, 4, c1, 2, (1 - odd) * (rows - 2), 2 - 4 * odd, 2, every)
    advance(c1, 2, out, 0, 4 - 4 * odd, 2, (rows - 4) // 2, every)

    @pl.when(has_slow)
    def _():
        for d in range(1, members):
            relay_copy(0, d, lax.rem(member + members - d, members)).wait_recv()

    halo_coefficients(0)

    def last(m, carry):
        @pl.when(has_slow)
        def _():
            slow_arrival(m, 0).wait_recv()

        advance(c0, 4, c1, 2, odd * (rows - 2), 2, 1, [m])
        advance(c1, 2, out, 0, 2 + odd * (rows - 6), 2, 1, [m])

        @pl.when(has_slow)
        def _():
            slow_arrival(m, 1).wait_recv()

        advance(c0, 4, c1, 2, odd * (rows + 2) - 2, 2, 1, [m])
        advance(c1, 2, out, 0, odd * (rows - 2), 2, 1, [m])
        return carry

    lax.fori_loop(0, local_m, last, 0)

    for d in range(1, members):
        hy_copy(d, member).wait_send()
        relay_copy(1, d, member).wait_send()
    stage_copy(1).wait_send()
    for m in every:
        for far in range(2):
            fast_copy(m, far).wait_send()

    @pl.when(has_slow)
    def _():
        stage_copy(0).wait_send()
        for d in range(1, members):
            relay_copy(0, d, member).wait_send()
        for m in every:
            for far in range(2):
                slow_copy(m, far).wait_send()


def on_device(members, tiles, tracers, hydro, wet, rates, decays):
    local_m, count, layers, rows, cols = tracers.shape
    tiles_c = cols // LANE
    pairs = tiles_c // 2
    groups = local_m * count
    conc = tracers.transpose(0, 1, 3, 2, 4).reshape(local_m, count, rows, layers, tiles_c, LANE)
    conc = conc.transpose(0, 1, 2, 4, 3, 5).reshape(groups, rows, pairs, SUB, LANE)
    planes = hydro.transpose(1, 0, 2)
    coupling = rates.transpose(1, 0, 2)
    dma = pltpu.SemaphoreType.DMA
    wide = count * SUB
    depth = planes.shape[1]
    others = max(members - 1, 1)
    f32 = jnp.float32
    result = pl.pallas_call(
        functools.partial(kernel, members, tiles),
        out_shape=jax.ShapeDtypeStruct(conc.shape, f32),
        in_specs=[pl.BlockSpec(memory_space=pltpu.HBM)] * 5,
        out_specs=pl.BlockSpec(memory_space=pltpu.VMEM),
        scratch_shapes=[
            pltpu.VMEM((groups, rows + 8, pairs, SUB, LANE), f32),
            pltpu.VMEM((groups, rows + 4, pairs, SUB, LANE), f32),
            pltpu.VMEM((members, rows, depth, LANE), f32),
            pltpu.VMEM(wet.shape, wet.dtype),
            pltpu.VMEM(coupling.shape, f32),
            pltpu.VMEM(decays.shape, f32),
            pltpu.VMEM((2, 2, depth + 1, LANE), f32),
            pltpu.VMEM((2, members, 2, depth + 1, LANE), f32),
            pltpu.VMEM((rows, pairs, SUB, LANE), f32),
            pltpu.VMEM((rows + 4, pairs, 10, SUB, LANE), f32),
            pltpu.VMEM((local_m, wide, 2 * wide), jnp.bfloat16),
            pltpu.VMEM((local_m, wide, wide), jnp.bfloat16),
            pltpu.VMEM((groups, SUB, LANE), f32),
            dma((5,)),
            dma((2 * local_m,)), dma((2 * local_m,)),
            dma((2 * local_m,)), dma((2 * local_m,)),
            dma((others,)), dma((others,)),
            dma((2,)), dma((2,)),
            dma((2 * others,)), dma((2 * others,)),
        ],
        compiler_params=pltpu.CompilerParams(
            collective_id=0, has_side_effects=True, vmem_limit_bytes=48 * 1024 * 1024
        ),
    )(*(pltpu.with_memory_space_constraint(x, pltpu.HBM) for x in (conc, planes, wet, coupling, decays)))
    result = result.reshape(local_m, count, rows, tiles_c, layers, LANE).transpose(0, 1, 2, 4, 3, 5)
    return result.reshape(local_m, count, rows, layers, cols).transpose(0, 1, 3, 2, 4)


def solution(mesh):
    placed = (
        P("member", None, None, "tile", None),
        P(None, "tile", "member"),
        P("tile", None),
        P("member", None, None),
        P("member", None),
    )
    return jax.shard_map(
        functools.partial(on_device, mesh.shape["member"], mesh.shape["tile"]),
        mesh=mesh,
        in_specs=placed,
        out_specs=P("member", None, None, "tile", None),
        check_vma=False,
    )
```

time: 21.1 us -> 18.3 us (0.87)
  local copies, waits for them, and re-layouts: 5.28 us -> 1.02 us
  Pallas kernels: 15.5 us -> 17 us
    unnamed x10 -> x1, local copies, waits for them, and re-layouts: 5.28 us -> 1.02 us
    pallas_call x1, Pallas kernels: 15.5 us -> 17 us  [on_device(): pl.pallas_call(functools.partial(kernel, members, tiles), out_shape=jax.S...]
where the time goes in v2:
time: 18.3 us; the launch traced here: 18 us
  Pallas kernels  17 us (93%)
  local copies, waits for them, and re-layouts  1.02 us (6%)
    pallas_call x1, Pallas kernels, on_device(): pl.pallas_call(functools.partial(kernel, members, tiles), out_shape=jax.S...  17 us
    unnamed x1, local copies, waits for them, and re-layouts  1.02 us

profile of v2, /device:TPU:17, one launch (start us, length us, event | category | flops | bytes accessed | tf_op | source)
XLA Modules:
  0.0 18.0 jit_solution(8827459829057670349)
XLA Ops:
  0.0 17.0 %shard_map.55 = f32[24,12,1,8,128]{4,3,2,1,0:T(8,128)S(1)} custom-call(f32[24,12,1,8,128]{4,3,2,1,0:T(8,128)} %bitcast.17, f32[12,15,128]{2,1,0:T(8,128)} %bitcast.18, s32[12,256]{1,0:T(8,128)} %wet_in.1, f32[12,2,12]{2,1,0:T(2,128)} %bitcast.19, f32[2,12]{1,0:T(2,128)} %decays_in.1), custom_call_target="tpu_custom_call" | custom-call | tf_op jit(solution)/shard_map/pallas_call | solution.py:370
  17.0 1.0 %copy.8 = f32[2,12,4,12,256]{4,2,3,1,0:T(4,128)} copy(f32[2,12,4,12,256]{4,2,3,1,0:T(4,128)S(1)} %bitcast.16) | data formatting | bytes 2359296

commit v3 on v2

--- a/solution.py
+++ b/solution.py
@@ -41,7 +41,8 @@
     def _():
         greet(slow_id)
 
-    greet(fast_id)
+    for d in range(members):
+        greet({"tile": fast_tile, "member": other(d)})
     for d in range(1, members):
         greet({"tile": tile, "member": other(d)})
 
@@ -95,32 +96,21 @@
             hyin, hy.at[slot], hy_send.at[d - 1], hy_recv.at[d - 1], {"tile": tile, "member": other(d)}
         )
 
-    def stage_copy(side):
+    slow_stage = remote(
+        stage.at[0], hx.at[0, member], stage_send.at[members], stage_recv.at[members], slow_id
+    )
+
+    def fast_stage(d, slot):
         return remote(
-            stage.at[side], hx.at[side, member], stage_send.at[side], stage_recv.at[side],
-            (slow_id, fast_id)[side],
+            stage.at[1], hx.at[1, slot], stage_send.at[d], stage_recv.at[d],
+            {"tile": fast_tile, "member": other(d)},
         )
 
-    def relay_copy(side, d, slot):
-        k = side * max(members - 1, 1) + d - 1
+    def relay_copy(d, slot):
         return remote(
-            hx.at[side, slot], hx.at[side, slot], relay_send.at[k], relay_recv.at[k],
+            hx.at[0, slot], hx.at[0, slot], relay_send.at[d - 1], relay_recv.at[d - 1],
             {"tile": tile, "member": other(d)},
         )
-
-    pl.semaphore_wait(barrier, members + has_slow.astype(jnp.int32))
-
-    @pl.when(has_slow)
-    def _():
-        for m in range(local_m):
-            for far in range(2):
-                slow_copy(m, far).start()
-
-    for d in range(1, members):
-        hy_copy(d, member).start()
-    for m in range(local_m):
-        for far in range(2):
-            fast_copy(m, far).start()
 
     loads[0].wait()
     loads[1].wait()
@@ -139,11 +129,26 @@
             stage[side, j, 0:15] = hy[member, first + j]
             stage[side, j, 15:16] = jnp.where(low_side, low_row, high_row)
 
-    @pl.when(has_slow)
-    def _():
-        stage_copy(0).start()
-
-    stage_copy(1).start()
+    pl.semaphore_wait(barrier, 2 * members - 1 + has_slow.astype(jnp.int32))
+
+    @pl.when(has_slow)
+    def _():
+        slow_stage.start()
+
+    for d in range(1, members):
+        hy_copy(d, member).start()
+
+    @pl.when(has_slow)
+    def _():
+        for m in range(local_m):
+            for far in range(2):
+                slow_copy(m, far).start()
+
+    for d in range(members):
+        fast_stage(d, member).start()
+    for m in range(local_m):
+        for far in range(2):
+            fast_copy(m, far).start()
 
     @pl.when(jnp.logical_not(has_slow))
     def _():
@@ -290,22 +295,17 @@
     every = list(range(local_m))
     advance(c0, 4, c1, 2, 2, 2, (rows - 4) // 2, every)
 
-    def relay(side):
-        stage_copy(side).wait_recv()
+    @pl.when(has_slow)
+    def _():
+        slow_stage.wait_recv()
         for d in range(1, members):
-            relay_copy(side, d, member).start()
-
-    relay(1)
-
-    @pl.when(has_slow)
-    def _():
-        relay(0)
+            relay_copy(d, member).start()
 
     for m in every:
         for far in range(2):
             fast_arrival(m, far).wait_recv()
-    for d in range(1, members):
-        relay_copy(1, d, lax.rem(member + members - d, members)).wait_recv()
+    for d in range(members):
+        fast_stage(d, lax.rem(member + members - d, members)).wait_recv()
     halo_coefficients(1)
     advance(c0, 4, c1, 2, (1 - odd) * (rows - 2), 2 - 4 * odd, 2, every)
     advance(c1, 2, out, 0, 4 - 4 * odd, 2, (rows - 4) // 2, every)
@@ -313,7 +313,7 @@
     @pl.when(has_slow)
     def _():
         for d in range(1, members):
-            relay_copy(0, d, lax.rem(member + members - d, members)).wait_recv()
+            relay_copy(d, lax.rem(member + members - d, members)).wait_recv()
 
     halo_coefficients(0)
 
@@ -337,17 +337,17 @@
 
     for d in range(1, members):
         hy_copy(d, member).wait_send()
-        relay_copy(1, d, member).wait_send()
-    stage_copy(1).wait_send()
+    for d in range(members):
+        fast_stage(d, member).wait_send()
     for m in every:
         for far in range(2):
             fast_copy(m, far).wait_send()
 
     @pl.when(has_slow)
     def _():
-        stage_copy(0).wait_send()
+        slow_stage.wait_send()
         for d in range(1, members):
-            relay_copy(0, d, member).wait_send()
+            relay_copy(d, member).wait_send()
         for m in every:
             for far in range(2):
                 slow_copy(m, far).wait_send()
@@ -390,8 +390,8 @@
             dma((2 * local_m,)), dma((2 * local_m,)),
             dma((2 * local_m,)), dma((2 * local_m,)),
             dma((others,)), dma((others,)),
-            dma((2,)), dma((2,)),
-            dma((2 * others,)), dma((2 * others,)),
+            dma((members + 1,)), dma((members + 1,)),
+            dma((others,)), dma((others,)),
         ],
         compiler_params=pltpu.CompilerParams(
             collective_id=0, has_side_effects=True, vmem_limit_bytes=48 * 1024 * 1024

time: 18.3 us -> 14.6 us (0.80)
  Pallas kernels: 17 us -> 13.4 us
    pallas_call x1, Pallas kernels: 17 us -> 13.4 us  [on_device(): pl.pallas_call(functools.partial(kernel, members, tiles), out_shape=jax.S...]
where the time goes in v3:
time: 14.6 us; the launch traced here: 14.4 us
  Pallas kernels  13.4 us (92%)
  local copies, waits for them, and re-layouts  1.02 us (7%)
    pallas_call x1, Pallas kernels, on_device(): pl.pallas_call(functools.partial(kernel, members, tiles), out_shape=jax.S...  13.4 us
    unnamed x1, local copies, waits for them, and re-layouts  1.02 us

profile of v3, /device:TPU:17, one launch (start us, length us, event | category | flops | bytes accessed | tf_op | source)
XLA Modules:
  0.0 14.4 jit_solution(12482832447186048007)
XLA Ops:
  0.0 13.4 %shard_map.55 = f32[24,12,1,8,128]{4,3,2,1,0:T(8,128)S(1)} custom-call(f32[24,12,1,8,128]{4,3,2,1,0:T(8,128)} %bitcast.17, f32[12,15,128]{2,1,0:T(8,128)} %bitcast.18, s32[12,256]{1,0:T(8,128)} %wet_in.1, f32[12,2,12]{2,1,0:T(2,128)} %bitcast.19, f32[2,12]{1,0:T(2,128)} %decays_in.1), custom_call_target="tpu_custom_call" | custom-call | tf_op jit(solution)/shard_map/pallas_call | solution.py:370
  13.4 1.0 %copy.8 = f32[2,12,4,12,256]{4,2,3,1,0:T(4,128)} copy(f32[2,12,4,12,256]{4,2,3,1,0:T(4,128)S(1)} %bitcast.16) | data formatting | bytes 2359296
